TPU v7x, 32 devices: a whole 2x2x4 slice. The times are simulated.
32 devices in a mesh: seq: 16 (over z, x, core), wshard: 2 (over y).
Axes of the slice: x: 2, y: 2, z: 4, core: 2. Of those that a mesh axis runs over, the one named last changes fastest.
Arguments:
- hidden: bfloat16 [8, 2048, 1024], P('wshard', 'seq'), may hold values from -6 to 6
- segments: int32 [8, 2048], P('wshard', 'seq'), may hold values from 0 to 2, never falling along the last dimension, each value on 1 to 1536 neighbouring positions
- cotangent: bfloat16 [8, 2048, 1024], P('wshard', 'seq'), may hold values from -6 to 6
- in_weight: bfloat16 [1024, 3, 1024], P(None, None, 'wshard'), may hold values from -0.1875 to 0.1875
- out_weight: bfloat16 [1024, 1024], P('wshard'), may hold values from -0.1875 to 0.1875
- gate_weight: bfloat16 [1024, 4608], P(None, 'wshard'), may hold values from -0.1875 to 0.1875
- up_weight: bfloat16 [1024, 4608], P(None, 'wshard'), may hold values from -0.1875 to 0.1875
- down_weight: bfloat16 [4608, 1024], P('wshard'), may hold values from -0.09375 to 0.09375
- conv_weight: bfloat16 [3, 1024], P(None, 'wshard'), may hold values from -3 to 3
- norm_mix: bfloat16 [1024], P('wshard'), may hold values from 0.5 to 1.5
- norm_ffn: bfloat16 [1024], P('wshard'), may hold values from 0.5 to 1.5
Outputs:
- block_out: bfloat16 [8, 2048, 1024], P('wshard', 'seq')
- grad_hidden: float32 [8, 2048, 1024], P('wshard', 'seq')
- grad_in: float32 [1024, 3, 1024], P('seq', None, 'wshard')
- grad_out: float32 [1024, 1024], P('wshard', 'seq')
- grad_gate: float32 [1024, 4608], P('seq', 'wshard')
- grad_up: float32 [1024, 4608], P('seq', 'wshard')
- grad_down: float32 [4608, 1024], P('wshard', 'seq')
- grad_conv: float32 [3, 1024], P(None, 'wshard')
- grad_norm_mix: float32 [1024], P('wshard')
- grad_norm_ffn: float32 [1024], P('wshard')
Inputs may be any that keep to these rules, and one draw needn't show every extreme that they name: `segments`: segment numbers never fall along a sequence; each document holds 1 to 1536 tokens, one exactly that many.
All inputs are finite; a program needn't handle non-finite values.
Results may differ from a plain program's by a relative error of at most 0.017.
Values may be sent and summed in bfloat16 or wider, within the bound.
No kernel may reach another device: no remote copies, remote signals or barrier semaphores. Data moves between devices by JAX's collectives and lax.ppermute only.
A program may use at most 256 MiB of HBM per device.

v0:
```python
import jax
import jax.numpy as jnp
from jax import lax
from jax.sharding import PartitionSpec as P

EPS = 1e-05
LOW = jnp.bfloat16
F32 = jnp.float32


def over_seq(block, route):
    return lax.ppermute(block, "seq", route)


def swap_seq(block, mask):
    return over_seq(block, [(i, i ^ mask) for i in range(lax.axis_size("seq"))])


def swap_core(block):
    return swap_seq(block, 1)


def swap_pair(block):
    return lax.ppermute(block, "wshard", [(0, 1), (1, 0)])


def swap(block, link):
    return swap_pair(block) if link == "pair" else swap_seq(block, 2 * link)


def mm(left, right):
    return jnp.dot(left, right, preferred_element_type=F32)


def mm_tn(left, right):
    return lax.dot_general(left, right, (((0,), (0,)), ((), ())), preferred_element_type=F32)


def mm_nt(left, right):
    return lax.dot_general(left, right, (((1,), (1,)), ((), ())), preferred_element_type=F32)


def norm_stats(values):
    return lax.rsqrt(jnp.mean(values * values, axis=-1, keepdims=True) + EPS)


def norm_back(upstream, values, scale, gain):
    scaled = values * scale
    weighted = upstream * gain
    inner = jnp.mean(weighted * scaled, axis=-1, keepdims=True)
    return scale * (weighted - scaled * inner)


def slot_masks(order):
    masks = [0]
    for link in reversed(order):
        masks = masks + [mask ^ link for mask in masks]
    return masks


def in_slots(grad, chip, order):
    chips = lax.axis_size("seq") // 2
    blocks = grad.astype(LOW).reshape(chips, grad.shape[0] // chips, grad.shape[1])
    return jnp.stack(
        [lax.dynamic_index_in_dim(blocks, chip ^ mask, 0, False) for mask in slot_masks(order)]
    )


def halving(send, keep, order):
    terms = [keep]
    half = keep.shape[0]
    terms.append(swap(send, order[0]))
    for link in order[1:]:
        half //= 2
        going = sum((term[half : 2 * half].astype(F32) for term in terms)).astype(LOW)
        terms.append(swap(going, link))
    return sum((term[0].astype(F32) for term in terms))


def scatter_seq(grad, chip, order):
    slots = in_slots(grad, chip, order)
    half = slots.shape[0] // 2
    return halving(slots[half:], slots[:half], order)


def scatter_all(mine, other, chip, order):
    return halving(in_slots(other, chip, order[1:]), in_slots(mine, chip, order[1:]), order)


def local(
    hidden,
    segments,
    cotangent,
    in_weight,
    out_weight,
    gate_weight,
    up_weight,
    down_weight,
    conv_weight,
    norm_mix,
    norm_ffn,
):
    groups, block, width = hidden.shape
    rows = groups * block
    size = lax.axis_size("seq")
    seq_index = lax.axis_index("seq")
    core = seq_index % 2
    chip = seq_index // 2
    pair = lax.axis_index("wshard")
    first_core = core == 0
    chips = size // 2
    links = [1 << bit for bit in range(chips.bit_length() - 1)]
    features = out_weight.shape[0] // 2
    units = gate_weight.shape[1] // 2

    def ordered(flag, mine, other, axis):
        return jnp.where(
            flag,
            jnp.concatenate([mine, other], axis=axis),
            jnp.concatenate([other, mine], axis=axis),
        )

    small = jnp.concatenate([conv_weight, norm_mix[None], norm_ffn[None]], axis=0)
    small_other = swap_pair(small)
    gains = ordered(pair == 0, small[3:], small_other[3:], 1).astype(F32)
    gain_mix, gain_ffn = (gains[0], gains[1])

    def of_core(array, axis):
        return lax.dynamic_slice_in_dim(
            array, core * (array.shape[axis] // 2), array.shape[axis] // 2, axis
        )

    taps = jnp.concatenate([of_core(small[:3], 1), of_core(small_other[:3], 1)], axis=1).astype(F32)
    in_mine = of_core(jnp.transpose(in_weight, (1, 0, 2)), 2)
    in_other = swap_pair(in_mine)
    out_mine = of_core(out_weight, 0)
    out_other = swap_pair(out_mine)
    in_mat = jnp.concatenate([part for j in range(3) for part in (in_mine[j], in_other[j])], axis=1)
    out_mat = jnp.concatenate([out_mine, out_other], axis=0)
    conv_width = 2 * features
    own = hidden.reshape(rows, width)
    chip_hidden = jnp.concatenate([own, swap_core(own)], axis=0)
    seg_low = segments.astype(LOW)
    seg_other = swap_core(segments)
    edge = jnp.concatenate(
        [hidden, jnp.broadcast_to(seg_low[:, :, None], (groups, block, 128))], axis=2
    )
    last, head = (edge[:, block - 2 :], edge[:, :2])
    odd = range(1, size - 1, 2)
    even = range(2, size, 2)
    before = jnp.where(
        first_core,
        over_seq(last, [(i, i + 1) for i in odd]),
        over_seq(last, [(i, i + 2) for i in odd]),
    )
    after = jnp.where(
        first_core,
        over_seq(head, [(i, i - 2) for i in even]),
        over_seq(head, [(i, i - 1) for i in even]),
    )
    edges = jnp.concatenate([before, after], axis=0)
    edge_hidden = edges[:, :, :width].reshape(4 * groups, width)
    edge_segs = edges[:, :, width].astype(jnp.int32)
    resid = chip_hidden.astype(F32)
    scale_mix = norm_stats(resid)
    normed_mix = (resid * scale_mix * gain_mix).astype(LOW)
    edge_resid = edge_hidden.astype(F32)
    edge_normed = (edge_resid * norm_stats(edge_resid) * gain_mix).astype(LOW)
    projected = mm(normed_mix, in_mat)
    edge_projected = mm(edge_normed, in_mat)
    b_part = projected[:, :conv_width]
    c_part = projected[:, conv_width : 2 * conv_width]
    x_part = projected[:, 2 * conv_width :]

    def by_core(array):
        return array.reshape((2, groups, block) + array.shape[1:])

    def lead(own_lead, other_lead):
        return jnp.stack([own_lead, other_lead])

    conv_in = by_core((b_part * x_part).astype(LOW).astype(F32))
    edge_conv_in = (
        (edge_projected[: 2 * groups, :conv_width] * edge_projected[: 2 * groups, 2 * conv_width :])
        .astype(LOW)
        .astype(F32)
        .reshape(groups, 2, conv_width)
    )
    edge_c = edge_projected[2 * groups :, conv_width : 2 * conv_width]
    segs = jnp.stack([segments, seg_other])
    segs_before, segs_after = (edge_segs[:groups], edge_segs[groups:])

    def with_before(values, outside):
        ahead = jnp.where(
            first_core,
            lead(outside, values[0, :, block - 2 :]),
            lead(values[1, :, block - 2 :], outside),
        )
        return jnp.concatenate([ahead, values], axis=2)

    def with_after(values, outside):
        behind = jnp.where(
            first_core, lead(values[1, :, :2], outside), lead(outside, values[0, :, :2])
        )
        return jnp.concatenate([values, behind], axis=2)

    ext = with_before(conv_in, edge_conv_in)
    segs_ext = with_before(segs, segs_before)
    keep_one = (segs_ext[:, :, 1 : 1 + block] == segs).astype(F32)[..., None]
    keep_two = (segs_ext[:, :, :block] == segs).astype(F32)[..., None]
    lag_one = keep_one * ext[:, :, 1 : 1 + block]
    lag_two = keep_two * ext[:, :, :block]
    conv_out = (taps[2] * conv_in + taps[1] * lag_one + taps[0] * lag_two).reshape(
        2 * rows, conv_width
    )
    mixed = (c_part * conv_out).astype(LOW)
    mix_part = mm(mixed, out_mat).astype(LOW)
    mix_other = swap_core(mix_part)
    mix_term = mix_part.astype(F32) + jnp.concatenate(
        [mix_other[rows:], mix_other[:rows]], axis=0
    ).astype(F32)
    resid_two = resid + mix_term
    scale_ffn = norm_stats(resid_two)
    normed_ffn = (resid_two * scale_ffn * gain_ffn).astype(LOW)

    def gathered(mine):
        far = swap_pair(mine)
        return (far, swap_core(far))

    cot = cotangent.reshape(rows, width)
    cot_chip = jnp.concatenate([cot, swap_core(cot)], axis=0)
    cot_far = jnp.concatenate(gathered(cot), axis=0)
    normed_far = jnp.concatenate(gathered(normed_ffn[:rows]), axis=0)
    gate_mat = of_core(gate_weight, 1)
    up_mat = of_core(up_weight, 1)
    down_mat = of_core(down_weight, 0)

    def feed_forward(normed, upstream):
        gate = mm(normed, gate_mat)
        up_value = mm(normed, up_mat)
        d_act = mm_nt(upstream, down_mat)
        sigma = jax.nn.sigmoid(gate)
        silu_gate = gate * sigma
        act = (silu_gate * up_value).astype(LOW)
        d_gate = (d_act * up_value * sigma * (1.0 + gate * (1.0 - sigma))).astype(LOW)
        d_up = (d_act * silu_gate).astype(LOW)
        term = mm(act, down_mat).astype(LOW)
        d_normed = (mm_nt(d_gate, gate_mat) + mm_nt(d_up, up_mat)).astype(LOW)
        return (act, d_gate, d_up, term, d_normed)

    near_out = feed_forward(normed_ffn, cot_chip)
    far_out = feed_forward(normed_far, cot_far)

    def home(near, far):
        near_sum = near[:rows].astype(F32) + swap_core(near[rows:]).astype(F32)
        far_sum = (far[:rows].astype(F32) + swap_core(far[rows:]).astype(F32)).astype(LOW)
        return near_sum + swap_pair(far_sum).astype(F32)

    d_normed_ffn = home(near_out[4], far_out[4])
    block_out = (resid_two[:rows] + home(near_out[3], far_out[3])).astype(LOW)
    all_normed = jnp.concatenate([normed_ffn, normed_far], axis=0)
    all_cot = jnp.concatenate([cot_chip, cot_far], axis=0)
    act, d_gate, d_up = (jnp.concatenate([near_out[i], far_out[i]], axis=0) for i in range(3))
    part_down = scatter_seq(mm_tn(all_cot, act), chip, links)
    part_gate = scatter_seq(mm_tn(all_normed, d_gate), chip, links)
    part_up = scatter_seq(mm_tn(all_normed, d_up), chip, links)
    upstream = cot.astype(F32)
    own_two, own_scale = (resid_two[:rows], scale_ffn[:rows])
    d_resid_two = upstream + norm_back(d_normed_ffn, own_two, own_scale, gain_ffn)
    grad_gain_ffn = jnp.sum(d_normed_ffn * own_two * own_scale, axis=0)
    d_resid_low = d_resid_two.astype(LOW)
    d_chip = jnp.concatenate([d_resid_low, swap_core(d_resid_low)], axis=0)
    d_head = d_resid_low.reshape(groups, block, width)[:, :2]
    d_after = jnp.where(
        first_core,
        over_seq(d_head, [(i, i - 2) for i in even]),
        over_seq(d_head, [(i, i - 1) for i in even]),
    ).reshape(2 * groups, width)
    d_mixed = mm_nt(d_chip, out_mat)
    edge_d_conv = (mm_nt(d_after, out_mat) * edge_c).reshape(groups, 2, conv_width)
    d_conv = by_core(d_mixed * c_part)
    d_c = d_mixed * conv_out
    grad_taps = jnp.stack(
        [
            jnp.sum(d_conv * lag_two, axis=(0, 1, 2)),
            jnp.sum(d_conv * lag_one, axis=(0, 1, 2)),
            jnp.sum(d_conv * conv_in, axis=(0, 1, 2)),
        ]
    )
    d_ext = with_after(d_conv, edge_d_conv)
    segs_next = with_after(segs, segs_after)
    next_one = (segs_next[:, :, 1 : 1 + block] == segs).astype(F32)[..., None]
    next_two = (segs_next[:, :, 2 : 2 + block] == segs).astype(F32)[..., None]
    d_conv_in = (
        taps[2] * d_conv
        + taps[1] * next_one * d_ext[:, :, 1 : 1 + block]
        + taps[0] * next_two * d_ext[:, :, 2 : 2 + block]
    ).reshape(2 * rows, conv_width)
    d_proj = jnp.concatenate([d_conv_in * x_part, d_c, d_conv_in * b_part], axis=1).astype(LOW)
    grad_out = mm_tn(d_chip, mixed)
    grad_in = mm_tn(normed_mix, d_proj)
    d_normed_part = mm_nt(d_proj, in_mat).astype(LOW)
    d_normed_mix = d_normed_part[:rows].astype(F32) + swap_core(d_normed_part[rows:]).astype(F32)
    own_resid, own_mix = (resid[:rows], scale_mix[:rows])
    grad_hidden = (d_resid_two + norm_back(d_normed_mix, own_resid, own_mix, gain_mix)).reshape(
        groups, block, width
    )
    grad_gain_mix = jnp.sum(d_normed_mix * own_resid * own_mix, axis=0)
    halves = [grad_out] + [grad_in[:, j * conv_width : (j + 1) * conv_width] for j in range(3)]
    mixed_mine = jnp.concatenate([half[:, :features] for half in halves], axis=1)
    mixed_far = jnp.concatenate([half[:, features:] for half in halves], axis=1)
    part_mix = scatter_all(mixed_mine, mixed_far, chip, ["pair"] + links)
    part_rows = width // size

    def finish(part):
        low = part.astype(LOW).reshape(2, part_rows, -1)
        came = swap_core(lax.dynamic_index_in_dim(low, 1 - core, 0, False)).astype(F32)
        mine = lax.dynamic_index_in_dim(part.reshape(2, part_rows, -1), core, 0, False)
        return (mine, came)

    def wide(part):
        mine, came = finish(part)
        return ordered(first_core, mine, came, 1)

    out_down = wide(part_down).T
    out_gate = wide(part_gate)
    out_up = wide(part_up)
    mix_mine, mix_came = finish(part_mix)
    mix_parts = [
        ordered(
            first_core,
            mix_mine[:, j * features : (j + 1) * features],
            mix_came[:, j * features : (j + 1) * features],
            1,
        )
        for j in range(4)
    ]
    out_out = mix_parts[0].T
    out_in = jnp.stack(mix_parts[1:], axis=1)
    half_width = norm_mix.shape[0]
    spread = jnp.zeros((3, width), F32)
    spread = lax.dynamic_update_slice_in_dim(
        spread, grad_taps[:, :features], pair * half_width + core * features, 1
    )
    spread = lax.dynamic_update_slice_in_dim(
        spread, grad_taps[:, features:], (1 - pair) * half_width + core * features, 1
    )
    sums = lax.psum(
        jnp.concatenate([spread, grad_gain_mix[None], grad_gain_ffn[None]], axis=0),
        ("seq", "wshard"),
    )
    sums = lax.dynamic_slice_in_dim(sums, pair * half_width, half_width, 1)
    return (
        block_out.reshape(groups, block, width),
        grad_hidden,
        out_in,
        out_out,
        out_gate,
        out_up,
        out_down,
        sums[:3],
        sums[3],
        sums[4],
    )


def solution(mesh):
    return jax.shard_map(
        local,
        mesh=mesh,
        in_specs=(
            P("wshard", "seq", None),
            P("wshard", "seq"),
            P("wshard", "seq", None),
            P(None, None, "wshard"),
            P("wshard", None),
            P(None, "wshard"),
            P(None, "wshard"),
            P("wshard", None),
            P(None, "wshard"),
            P("wshard"),
            P("wshard"),
        ),
        out_specs=(
            P("wshard", "seq", None),
            P("wshard", "seq", None),
            P("seq", None, "wshard"),
            P("wshard", "seq"),
            P("seq", "wshard"),
            P("seq", "wshard"),
            P("wshard", "seq"),
            P(None, "wshard"),
            P("wshard"),
            P("wshard"),
        ),
        check_vma=False,
    )
```

profile of v0, /device:TPU:0, one launch (start us, length us, event | category | flops | bytes accessed | tf_op | source)
XLA Modules:
  0.0 517.6 jit_solution(11000948463357092600)
XLA Ops:
  12.7 4.7 collective-permute-start.7
  21.6 25.2 %collective-permute-done.1 = bf16[5,512]{1,0:T(8,128)(2,1)S(1)} collective-permute-done((bf16[5,512]{1,0:T(8,128)(2,1)S(1)}, bf16[5,512]{1,0:T(8,128)(2,1)S(1)}, u32[]{:S(2)}, u32[]{:S(2)}) %collective-permute-start.1) | collective-permute-done | bytes 5152 | tf_op jit(solution)/shard_map/ppermute | solution.py:24
  63.7 5.4 %fusion.73 = f32[1024,1536]{1,0:T(8,128)S(1)} fusion(bf16[1024,1536]{1,0:T(8,128)(2,1)} %fusion.75, f32[1024]{0:T(1024)S(1)} %bitcast.190, f32[1024]{0:T(1024)S(1)} %add_rsqrt_fusion.1, bf16[512,1024]{1,0:T(8,128)(2,1)S(1)} %collective-permute-done, bf16[512,1024]{1,0:T(8,128)(2,1)S(1)} %bitcast.148), kind=kOutput, calls=%fused_computation.131 | convolution fusion | flops 3228565504 | bytes 11542528 | tf_op jit(solution)/shard_map/dot_general | solution.py:32
  73.1 4.2 convolution_convert_fusion.4
  79.7 23.4 %collective-permute-done.17 = bf16[512,1024]{1,0:T(8,128)(2,1)} collective-permute-done((bf16[512,1024]{1,0:T(8,128)(2,1)}, bf16[512,1024]{1,0:T(8,128)(2,1)}, u32[]{:S(2)}, u32[]{:S(2)}) %collective-permute-start.17) | collective-permute-done | bytes 1048608 | tf_op jit(solution)/shard_map/ppermute | solution.py:24
  113.5 4.5 fusion.61
  118.0 4.5 fusion.69
  122.6 9.7 %multiply_convert_fusion.2 = (bf16[1024,1152]{1,0:T(8,128)(2,1)S(1)}, bf16[1024,1152]{1,0:T(8,128)(2,1)}, bf16[1024,1152]{1,0:T(8,128)(2,1)}) fusion(f32[1024,1152]{1,0:T(8,128)} %fusion.69, f32[1024,1152]{1,0:T(8,128)} %fusion.61, bf16[2304,1024]{1,0:T(8,128)(2,1)S(1)} %bitcast.220, s32[]{:T(128)S(6)} %select_n.227, ...), kind=kOutput, calls=%fused_computation.14 | convolution fusion | flops 2437808128 | bytes 20971524 | tf_op jit(solution)/shard_map/dot_general | solution.py:40
  132.3 6.1 %fusion.65 = f32[1024,1024]{1,0:T(8,128)S(1)} fusion(bf16[1024,1152]{1,0:T(8,128)(2,1)} %get-tuple-element.24, bf16[1024,2304]{1,0:T(8,128)(2,1)} %param.16, s32[]{:T(128)S(6)} %select_n.227), kind=kOutput, calls=%fused_computation.113 | convolution fusion | flops 2415919104 | bytes 8912900 | tf_op jit(solution)/shard_map/dot_general | solution.py:40
  138.8 5.0 add_convert_fusion.1
  149.6 4.5 fusion.59
  154.1 4.5 fusion.67
  158.6 11.4 %multiply_convert_fusion = (bf16[1024,1152]{1,0:T(8,128)(2,1)S(1)}, bf16[1024,1152]{1,0:T(8,128)(2,1)}, bf16[1024,1152]{1,0:T(8,128)(2,1)}) fusion(f32[1024,1152]{1,0:T(8,128)} %fusion.67, f32[1024,1152]{1,0:T(8,128)} %fusion.59, bf16[2304,1024]{1,0:T(8,128)(2,1)} %param.18, s32[]{:T(128)S(6)} %select_n.227, bf16[512,1024]{1,0:T(8,128)(2,1)} %collective-permute-done.18, ...), kind=kOutput, calls=%fused_computation.12 | convolution fusion | flops 2437808128 | bytes 20971524 | tf_op jit(solution)/shard_map/dot_general | solution.py:40
  170.1 6.1 %convolution_convert_fusion.1 = bf16[1024,1024]{1,0:T(8,128)(2,1)S(1)} fusion(bf16[1024,1152]{1,0:T(8,128)(2,1)} %get-tuple-element.28, bf16[2304,1024]{1,0:T(8,128)(2,1)} %param.18, s32[]{:T(128)S(6)} %select_n.227), kind=kOutput, calls=%fused_computation.96 | convolution fusion | flops 2416967680 | bytes 6815748 | tf_op jit(solution)/shard_map/dot_general | solution.py:32
  177.6 4.6 fusion.63
  187.7 9.3 %fusion.21 = bf16[1024,1152]{1,0:T(8,128)(2,1)S(1)} fusion(bf16[1024,1152]{1,0:T(8,128)(2,1)} %get-tuple-element.28, bf16[1024,1152]{1,0:T(8,128)(2,1)} %get-tuple-element.25, bf16[512,1024]{1,0:T(8,128)(2,1)} %collective-permute-done.18, bf16[512,1024]{1,0:T(8,128)(2,1)} %collective-permute-done.17, bf16[512,1024]{1,0:T(8,128)(2,1)} %collective-permute-done.15, ...), kind=kOutput, calls=%fused_computation.37 | convolution fusion | flops 4859232256 | bytes 11272192 | tf_op jit(solution)/shard_map/dot_general | solution.py:36
  199.9 8.2 %fusion.26 = bf16[1024,1152]{1,0:T(8,128)(2,1)S(1)} fusion(bf16[1024,1152]{1,0:T(8,128)(2,1)} %copy-done.38, bf16[1024,1152]{1,0:T(8,128)(2,1)} %copy-done.37, bf16[512,1024]{1,0:T(8,128)(2,1)S(1)} %collective-permute-done.12, bf16[512,1024]{1,0:T(8,128)(2,1)S(1)} %collective-permute-done.11, bf16[1024,1024]{1,0:T(8,128)(2,1)S(1)} %multiply_convert_fusion.6), kind=kOutput, calls=%fused_computation.38 | convolution fusion | flops 4855037952 | bytes 11272192 | tf_op jit(solution)/shard_map/dot_general | solution.py:36
  210.2 8.8 %fusion.29 = bf16[1024,1152]{1,0:T(8,128)(2,1)S(1)} fusion(bf16[1024,1152]{1,0:T(8,128)(2,1)} %get-tuple-element.27, bf16[1024,1152]{1,0:T(8,128)(2,1)} %get-tuple-element.24, bf16[512,1024]{1,0:T(8,128)(2,1)} %copy-done.24, bf16[512,1024]{1,0:T(8,128)(2,1)} %copy-done.23, bf16[1024,1024]{1,0:T(8,128)(2,1)S(1)} %multiply_convert_fusion.6), kind=kOutput, calls=%fused_computation.39 | convolution fusion | flops 4855037952 | bytes 11272192 | tf_op jit(solution)/shard_map/dot_general | solution.py:36
  229.3 23.5 %collective-permute-done.34 = bf16[4,128,1152]{2,1,0:T(8,128)(2,1)} collective-permute-done((bf16[4,128,1152]{2,1,0:T(8,128)(2,1)}, bf16[4,128,1152]{2,1,0:T(8,128)(2,1)}, u32[]{:S(2)}, u32[]{:S(2)}) %collective-permute-start.34) | collective-permute-done | bytes 1179680 | tf_op jit(solution)/shard_map/ppermute | solution.py:12
  255.6 21.7 %collective-permute-done.30 = bf16[4,128,1152]{2,1,0:T(8,128)(2,1)S(1)} collective-permute-done((bf16[4,128,1152]{2,1,0:T(8,128)(2,1)S(1)}, bf16[4,128,1152]{2,1,0:T(8,128)(2,1)S(1)}, u32[]{:S(2)}, u32[]{:S(2)}) %collective-permute-start.30) | collective-permute-done | bytes 1179680 | tf_op jit(solution)/shard_map/ppermute | solution.py:12
  280.6 12.9 %collective-permute-done.35 = bf16[2,128,1152]{2,1,0:T(8,128)(2,1)S(1)} collective-permute-done((bf16[2,128,1152]{2,1,0:T(8,128)(2,1)S(1)}, bf16[2,128,1152]{2,1,0:T(8,128)(2,1)S(1)}, u32[]{:S(2)}, u32[]{:S(2)}) %collective-permute-start.35) | collective-permute-done | bytes 589856 | tf_op jit(solution)/shard_map/ppermute | solution.py:12
  295.3 9.3 %collective-permute-done.31 = bf16[2,128,1152]{2,1,0:T(8,128)(2,1)S(1)} collective-permute-done((bf16[2,128,1152]{2,1,0:T(8,128)(2,1)S(1)}, bf16[2,128,1152]{2,1,0:T(8,128)(2,1)S(1)}, u32[]{:S(2)}, u32[]{:S(2)}) %collective-permute-start.31) | collective-permute-done | bytes 589856 | tf_op jit(solution)/shard_map/ppermute | solution.py:12
  307.3 11.9 %collective-permute-done.40 = bf16[1,128,1152]{2,1,0:T(8,128)(2,1)S(1)} collective-permute-done((bf16[1,128,1152]{2,1,0:T(8,128)(2,1)S(1)}, bf16[1,128,1152]{2,1,0:T(8,128)(2,1)S(1)}, u32[]{:S(2)}, u32[]{:S(2)}) %collective-permute-start.40) | collective-permute-done | bytes 294944 | tf_op jit(solution)/shard_map/ppermute | solution.py:12
  320.3 14.0 %collective-permute-done.36 = bf16[1,128,1152]{2,1,0:T(8,128)(2,1)S(1)} collective-permute-done((bf16[1,128,1152]{2,1,0:T(8,128)(2,1)S(1)}, bf16[1,128,1152]{2,1,0:T(8,128)(2,1)S(1)}, u32[]{:S(2)}, u32[]{:S(2)}) %collective-permute-start.36) | collective-permute-done | bytes 294944 | tf_op jit(solution)/shard_map/ppermute | solution.py:12
  336.9 11.6 %collective-permute-done.32 = bf16[1,128,1152]{2,1,0:T(8,128)(2,1)S(1)} collective-permute-done((bf16[1,128,1152]{2,1,0:T(8,128)(2,1)S(1)}, bf16[1,128,1152]{2,1,0:T(8,128)(2,1)S(1)}, u32[]{:S(2)}, u32[]{:S(2)}) %collective-permute-start.32) | collective-permute-done | bytes 294944 | tf_op jit(solution)/shard_map/ppermute | solution.py:12
  349.6 4.0 fusion.122
  366.2 4.6 multiply_reduce_fusion.6
  377.0 3.7 convolution_convert_fusion
  389.9 40.0 %collective-permute-done.25 = bf16[8,128,1024]{2,1,0:T(8,128)(2,1)S(1)} collective-permute-done((bf16[8,128,1024]{2,1,0:T(8,128)(2,1)S(1)}, bf16[8,128,1024]{2,1,0:T(8,128)(2,1)S(1)}, u32[]{:S(2)}, u32[]{:S(2)}) %collective-permute-start.25) | collective-permute-done | bytes 2097184 | tf_op jit(solution)/shard_map/ppermute | solution.py:24
  435.1 21.7 %collective-permute-done.26 = bf16[4,128,1024]{2,1,0:T(8,128)(2,1)S(1)} collective-permute-done((bf16[4,128,1024]{2,1,0:T(8,128)(2,1)S(1)}, bf16[4,128,1024]{2,1,0:T(8,128)(2,1)S(1)}, u32[]{:S(2)}, u32[]{:S(2)}) %collective-permute-start.26) | collective-permute-done | bytes 1048608 | tf_op jit(solution)/shard_map/ppermute | solution.py:12
  459.2 11.3 %collective-permute-done.27 = bf16[2,128,1024]{2,1,0:T(8,128)(2,1)S(1)} collective-permute-done((bf16[2,128,1024]{2,1,0:T(8,128)(2,1)S(1)}, bf16[2,128,1024]{2,1,0:T(8,128)(2,1)S(1)}, u32[]{:S(2)}, u32[]{:S(2)}) %collective-permute-start.27) | collective-permute-done | bytes 524320 | tf_op jit(solution)/shard_map/ppermute | solution.py:12
  471.4 40.1 %psum.7 = f32[5,1024]{1,0:T(8,128)S(1)} all-reduce(f32[5,1024]{1,0:T(8,128)S(1)} %pad_maximum_fusion.23), channel_id=1, replica_groups=mesh['seq'=16,'wshard'=2] {'seq','wshard'}, use_global_device_ids=true, to_apply=%region_10.11 | all-reduce | flops 5120 | bytes 40960 | tf_op jit(solution)/shard_map/psum | solution.py:347
  (342 shorter events, 135.0 us)
Async XLA Ops:
  5.7 41.8 %collective-permute-start.5 = (bf16[4,2,1152]{2,0,1:T(4,128)(2,1)S(1)}, bf16[4,2,1152]{2,0,1:T(4,128)(2,1)S(1)}, u32[]{:S(2)}, u32[]{:S(2)}) collective-permute-start(bf16[4,2,1152]{2,0,1:T(4,128)(2,1)S(1)} %get-tuple-element.69), channel_id=1, source_target_pairs={{4,0},{8,4},{12,8},{16,12},{20,16},{24,20},{28,24},{5,1},{9,5},{13... | collective-permute-start | bytes 55304 | tf_op jit(solution)/shard_map/ppermute | solution.py:12
  7.0 41.0 %collective-permute-start.6 = (bf16[4,2,1152]{2,0,1:T(4,128)(2,1)S(1)}, bf16[4,2,1152]{2,0,1:T(4,128)(2,1)S(1)}, u32[]{:S(2)}, u32[]{:S(2)}) collective-permute-start(bf16[4,2,1152]{2,0,1:T(4,128)(2,1)S(1)} %get-tuple-element.69), channel_id=1, source_target_pairs={{4,2},{8,6},{12,10},{16,14},{20,18},{24,22},{28,26},{5,3},{9,7},{1... | collective-permute-start | bytes 55304 | tf_op jit(solution)/shard_map/ppermute | solution.py:12
  9.0 42.0 %collective-permute-start.2 = (bf16[3,1024,256]{2,1,0:T(8,128)(2,1)}, bf16[3,1024,256]{2,1,0:T(8,128)(2,1)}, u32[]{:S(2)}, u32[]{:S(2)}) collective-permute-start(bf16[3,1024,256]{2,1,0:T(8,128)(2,1)} %dynamic-slice_bitcast_fusion), channel_id=1, source_target_pairs={{0,1},{1,0},{2,3},{3,2},{4,5},{5,4},{6,7},{7,6},{8,9},{9,8},{10,11... | collective-permute-start | bytes 4718600 | tf_op jit(solution)/shard_map/ppermute | solution.py:24
  11.9 37.5 %collective-permute-start.3 = (bf16[4,2,1152]{2,0,1:T(4,128)(2,1)S(1)}, bf16[4,2,1152]{2,0,1:T(4,128)(2,1)S(1)}, u32[]{:S(2)}, u32[]{:S(2)}) collective-permute-start(bf16[4,2,1152]{2,0,1:T(4,128)(2,1)S(1)} %get-tuple-element.68), channel_id=1, source_target_pairs={{2,4},{6,8},{10,12},{14,16},{18,20},{22,24},{26,28},{3,5},{7,9},{1... | collective-permute-start | bytes 55304 | tf_op jit(solution)/shard_map/ppermute | solution.py:12
  21.3 25.4 %collective-permute-start.1 = (bf16[5,512]{1,0:T(8,128)(2,1)S(1)}, bf16[5,512]{1,0:T(8,128)(2,1)S(1)}, u32[]{:S(2)}, u32[]{:S(2)}) collective-permute-start(bf16[5,512]{1,0:T(8,128)(2,1)S(1)} %pad_maximum_fusion.26), channel_id=1, source_target_pairs={{0,1},{1,0},{2,3},{3,2},{4,5},{5,4},{6,7},{7,6},{8,9},{9,8},{10,11... | collective-permute-start | bytes 15368 | tf_op jit(solution)/shard_map/ppermute | solution.py:24
  48.0 25.1 %collective-permute-start.8 = (bf16[256,1024]{1,0:T(8,128)(2,1)}, bf16[256,1024]{1,0:T(8,128)(2,1)}, u32[]{:S(2)}, u32[]{:S(2)}) collective-permute-start(bf16[256,1024]{1,0:T(8,128)(2,1)} %constant_dynamic-slice_fusion.25), channel_id=1, source_target_pairs={{0,1},{1,0},{2,3},{3,2},{4,5},{5,4},{6,7},{7,6},{8,9},{9,8},{10,11... | collective-permute-start | bytes 1572872 | tf_op jit(solution)/shard_map/ppermute | solution.py:24
  77.2 29.5 %collective-permute-start.9 = (bf16[1024,1024]{1,0:T(8,128)(2,1)}, bf16[1024,1024]{1,0:T(8,128)(2,1)}, u32[]{:S(2)}, u32[]{:S(2)}) collective-permute-start(bf16[1024,1024]{1,0:T(8,128)(2,1)} %convolution_convert_fusion.4), channel_id=1, source_target_pairs={{0,2},{2,0},{4,6},{6,4},{8,10},{10,8},{12,14},{14,12},{16,18},{18,... | collective-permute-start | bytes 6291464 | tf_op jit(solution)/shard_map/ppermute | solution.py:12
  77.5 25.7 %collective-permute-start.17 = (bf16[512,1024]{1,0:T(8,128)(2,1)}, bf16[512,1024]{1,0:T(8,128)(2,1)}, u32[]{:S(2)}, u32[]{:S(2)}) collective-permute-start(bf16[512,1024]{1,0:T(8,128)(2,1)} %bitcast.18), channel_id=1, source_target_pairs={{0,1},{1,0},{2,3},{3,2},{4,5},{5,4},{6,7},{7,6},{8,9},{9,8},{10,11... | collective-permute-start | bytes 3145736 | tf_op jit(solution)/shard_map/ppermute | solution.py:24
  78.9 43.6 %collective-permute-start.15 = (bf16[512,1024]{1,0:T(8,128)(2,1)}, bf16[512,1024]{1,0:T(8,128)(2,1)}, u32[]{:S(2)}, u32[]{:S(2)}) collective-permute-start(bf16[512,1024]{1,0:T(8,128)(2,1)} %bitcast.18), channel_id=1, source_target_pairs={{0,2},{2,0},{4,6},{6,4},{8,10},{10,8},{12,14},{14,12},{16,18},{18,... | collective-permute-start | bytes 3145736 | tf_op jit(solution)/shard_map/ppermute | solution.py:12
  103.1 55.5 %collective-permute-start.18 = (bf16[512,1024]{1,0:T(8,128)(2,1)}, bf16[512,1024]{1,0:T(8,128)(2,1)}, u32[]{:S(2)}, u32[]{:S(2)}) collective-permute-start(bf16[512,1024]{1,0:T(8,128)(2,1)} %collective-permute-done.17), channel_id=1, source_target_pairs={{0,2},{2,0},{4,6},{6,4},{8,10},{10,8},{12,14},{14,12},{16,18},{18,... | collective-permute-start | bytes 3145736 | tf_op jit(solution)/shard_map/ppermute | solution.py:12
  111.9 26.5 %collective-permute-start.11 = (bf16[512,1024]{1,0:T(8,128)(2,1)S(1)}, bf16[512,1024]{1,0:T(8,128)(2,1)S(1)}, u32[]{:S(2)}, u32[]{:S(2)}) collective-permute-start(bf16[512,1024]{1,0:T(8,128)(2,1)S(1)} %slice.503), channel_id=1, source_target_pairs={{0,1},{1,0},{2,3},{3,2},{4,5},{5,4},{6,7},{7,6},{8,9},{9,8},{10,11... | collective-permute-start | bytes 3145736 | tf_op jit(solution)/shard_map/ppermute | solution.py:24
  144.8 203.8 %collective-permute-start.16 = (bf16[512,1024]{1,0:T(8,128)(2,1)}, bf16[512,1024]{1,0:T(8,128)(2,1)S(1)}, u32[]{:S(2)}, u32[]{:S(2)}) collective-permute-start(bf16[512,1024]{1,0:T(8,128)(2,1)} %slice.507), channel_id=1, source_target_pairs={{0,2},{2,0},{4,6},{6,4},{8,10},{10,8},{12,14},{14,12},{16,18},{18,... | collective-permute-start | bytes 3145736 | tf_op jit(solution)/shard_map/ppermute | solution.py:12
  177.3 42.1 %collective-permute-start.13 = (bf16[512,1024]{1,0:T(8,128)(2,1)}, bf16[512,1024]{1,0:T(8,128)(2,1)}, u32[]{:S(2)}, u32[]{:S(2)}) collective-permute-start(bf16[512,1024]{1,0:T(8,128)(2,1)} %slice.505), channel_id=1, source_target_pairs={{0,2},{2,0},{4,6},{6,4},{8,10},{10,8},{12,14},{14,12},{16,18},{18,... | collective-permute-start | bytes 3145736 | tf_op jit(solution)/shard_map/ppermute | solution.py:12
  187.4 35.1 %collective-permute-start.19 = (bf16[512,1024]{1,0:T(8,128)(2,1)}, bf16[512,1024]{1,0:T(8,128)(2,1)}, u32[]{:S(2)}, u32[]{:S(2)}) collective-permute-start(bf16[512,1024]{1,0:T(8,128)(2,1)} %slice.509), channel_id=1, source_target_pairs={{0,2},{2,0},{4,6},{6,4},{8,10},{10,8},{12,14},{14,12},{16,18},{18,... | collective-permute-start | bytes 3145736 | tf_op jit(solution)/shard_map/ppermute | solution.py:12
  198.4 29.1 %collective-permute-start.38 = (bf16[4,128,1152]{2,1,0:T(8,128)(2,1)}, bf16[4,128,1152]{2,1,0:T(8,128)(2,1)}, u32[]{:S(2)}, u32[]{:S(2)}) collective-permute-start(bf16[4,128,1152]{2,1,0:T(8,128)(2,1)} %pad_maximum_fusion.16), channel_id=1, source_target_pairs={{0,4},{2,6},{4,0},{6,2},{8,12},{10,14},{12,8},{14,10},{16,20},{18,... | collective-permute-start | bytes 3538952 | tf_op jit(solution)/shard_map/ppermute | solution.py:12
  209.7 43.1 %collective-permute-start.34 = (bf16[4,128,1152]{2,1,0:T(8,128)(2,1)}, bf16[4,128,1152]{2,1,0:T(8,128)(2,1)}, u32[]{:S(2)}, u32[]{:S(2)}) collective-permute-start(bf16[4,128,1152]{2,1,0:T(8,128)(2,1)} %pad_maximum_fusion.15), channel_id=1, source_target_pairs={{0,4},{2,6},{4,0},{6,2},{8,12},{10,14},{12,8},{14,10},{16,20},{18,... | collective-permute-start | bytes 3538952 | tf_op jit(solution)/shard_map/ppermute | solution.py:12
  220.2 129.4 %collective-permute-start.10 = (bf16[512,1024]{1,0:T(8,128)(2,1)S(1)}, bf16[512,1024]{1,0:T(8,128)(2,1)S(1)}, u32[]{:S(2)}, u32[]{:S(2)}) collective-permute-start(bf16[512,1024]{1,0:T(8,128)(2,1)S(1)} %copy-done.22), channel_id=1, source_target_pairs={{0,2},{2,0},{4,6},{6,4},{8,10},{10,8},{12,14},{14,12},{16,18},{18,... | collective-permute-start | bytes 3145736 | tf_op jit(solution)/shard_map/ppermute | solution.py:12
  222.5 54.8 %collective-permute-start.30 = (bf16[4,128,1152]{2,1,0:T(8,128)(2,1)S(1)}, bf16[4,128,1152]{2,1,0:T(8,128)(2,1)S(1)}, u32[]{:S(2)}, u32[]{:S(2)}) collective-permute-start(bf16[4,128,1152]{2,1,0:T(8,128)(2,1)S(1)} %pad_maximum_fusion.14), channel_id=1, source_target_pairs={{0,4},{2,6},{4,0},{6,2},{8,12},{10,14},{12,8},{14,10},{16,20},{18,... | collective-permute-start | bytes 3538952 | tf_op jit(solution)/shard_map/ppermute | solution.py:12
  227.5 122.1 %collective-permute-start.14 = (bf16[512,1024]{1,0:T(8,128)(2,1)S(1)}, bf16[512,1024]{1,0:T(8,128)(2,1)S(1)}, u32[]{:S(2)}, u32[]{:S(2)}) collective-permute-start(bf16[512,1024]{1,0:T(8,128)(2,1)S(1)} %add_convert_fusion.5), channel_id=1, source_target_pairs={{0,1},{1,0},{2,3},{3,2},{4,5},{5,4},{6,7},{7,6},{8,9},{9,8},{10,11... | collective-permute-start | bytes 3145736 | tf_op jit(solution)/shard_map/ppermute | solution.py:24
  252.8 26.2 %collective-permute-start.39 = (bf16[2,128,1152]{2,1,0:T(8,128)(2,1)S(1)}, bf16[2,128,1152]{2,1,0:T(8,128)(2,1)S(1)}, u32[]{:S(2)}, u32[]{:S(2)}) collective-permute-start(bf16[2,128,1152]{2,1,0:T(8,128)(2,1)S(1)} %add_convert_fusion.6), channel_id=1, source_target_pairs={{0,8},{2,10},{4,12},{6,14},{8,0},{10,2},{12,4},{14,6},{16,24},{18,... | collective-permute-start | bytes 1769480 | tf_op jit(solution)/shard_map/ppermute | solution.py:12
  277.3 16.3 %collective-permute-start.35 = (bf16[2,128,1152]{2,1,0:T(8,128)(2,1)S(1)}, bf16[2,128,1152]{2,1,0:T(8,128)(2,1)S(1)}, u32[]{:S(2)}, u32[]{:S(2)}) collective-permute-start(bf16[2,128,1152]{2,1,0:T(8,128)(2,1)S(1)} %add_convert_fusion.7), channel_id=1, source_target_pairs={{0,8},{2,10},{4,12},{6,14},{8,0},{10,2},{12,4},{14,6},{16,24},{18,... | collective-permute-start | bytes 1769480 | tf_op jit(solution)/shard_map/ppermute | solution.py:12
  279.0 25.6 %collective-permute-start.31 = (bf16[2,128,1152]{2,1,0:T(8,128)(2,1)S(1)}, bf16[2,128,1152]{2,1,0:T(8,128)(2,1)S(1)}, u32[]{:S(2)}, u32[]{:S(2)}) collective-permute-start(bf16[2,128,1152]{2,1,0:T(8,128)(2,1)S(1)} %add_convert_fusion.8), channel_id=1, source_target_pairs={{0,8},{2,10},{4,12},{6,14},{8,0},{10,2},{12,4},{14,6},{16,24},{18,... | collective-permute-start | bytes 1769480 | tf_op jit(solution)/shard_map/ppermute | solution.py:12
  293.6 55.1 %collective-permute-start.20 = (bf16[512,1024]{1,0:T(8,128)(2,1)S(1)}, bf16[512,1024]{1,0:T(8,128)(2,1)S(1)}, u32[]{:S(2)}, u32[]{:S(2)}) collective-permute-start(bf16[512,1024]{1,0:T(8,128)(2,1)S(1)} %add_convert_fusion.3), channel_id=1, source_target_pairs={{0,1},{1,0},{2,3},{3,2},{4,5},{5,4},{6,7},{7,6},{8,9},{9,8},{10,11... | collective-permute-start | bytes 3145736 | tf_op jit(solution)/shard_map/ppermute | solution.py:24
  304.6 14.6 %collective-permute-start.40 = (bf16[1,128,1152]{2,1,0:T(8,128)(2,1)S(1)}, bf16[1,128,1152]{2,1,0:T(8,128)(2,1)S(1)}, u32[]{:S(2)}, u32[]{:S(2)}) collective-permute-start(bf16[1,128,1152]{2,1,0:T(8,128)(2,1)S(1)} %add_convert_fusion.10), channel_id=1, source_target_pairs={{0,16},{2,18},{4,20},{6,22},{8,24},{10,26},{12,28},{14,30},{16,0},... | collective-permute-start | bytes 884744 | tf_op jit(solution)/shard_map/ppermute | solution.py:12
  319.2 15.1 %collective-permute-start.36 = (bf16[1,128,1152]{2,1,0:T(8,128)(2,1)S(1)}, bf16[1,128,1152]{2,1,0:T(8,128)(2,1)S(1)}, u32[]{:S(2)}, u32[]{:S(2)}) collective-permute-start(bf16[1,128,1152]{2,1,0:T(8,128)(2,1)S(1)} %add_convert_fusion.11), channel_id=1, source_target_pairs={{0,16},{2,18},{4,20},{6,22},{8,24},{10,26},{12,28},{14,30},{16,0},... | collective-permute-start | bytes 884744 | tf_op jit(solution)/shard_map/ppermute | solution.py:12
  334.3 14.2 %collective-permute-start.32 = (bf16[1,128,1152]{2,1,0:T(8,128)(2,1)S(1)}, bf16[1,128,1152]{2,1,0:T(8,128)(2,1)S(1)}, u32[]{:S(2)}, u32[]{:S(2)}) collective-permute-start(bf16[1,128,1152]{2,1,0:T(8,128)(2,1)S(1)} %add_convert_fusion.12), channel_id=1, source_target_pairs={{0,16},{2,18},{4,20},{6,22},{8,24},{10,26},{12,28},{14,30},{16,0},... | collective-permute-start | bytes 884744 | tf_op jit(solution)/shard_map/ppermute | solution.py:12
  353.6 12.6 %collective-permute-start.21 = (bf16[512,1024]{1,0:T(8,128)(2,1)}, bf16[512,1024]{1,0:T(8,128)(2,1)}, u32[]{:S(2)}, u32[]{:S(2)}) collective-permute-start(bf16[512,1024]{1,0:T(8,128)(2,1)} %get-tuple-element.19), channel_id=1, source_target_pairs={{0,2},{2,0},{4,6},{6,4},{8,10},{10,8},{12,14},{14,12},{16,18},{18,... | collective-permute-start | bytes 3145736 | tf_op jit(solution)/shard_map/ppermute | solution.py:12
  381.5 48.4 %collective-permute-start.25 = (bf16[8,128,1024]{2,1,0:T(8,128)(2,1)S(1)}, bf16[8,128,1024]{2,1,0:T(8,128)(2,1)S(1)}, u32[]{:S(2)}, u32[]{:S(2)}) collective-permute-start(bf16[8,128,1024]{2,1,0:T(8,128)(2,1)S(1)} %dynamic-slice_dynamic-update-slice_fusion), channel_id=1, source_target_pairs={{0,1},{1,0},{2,3},{3,2},{4,5},{5,4},{6,7},{7,6},{8,9},{9,8},{10,11... | collective-permute-start | bytes 6291464 | tf_op jit(solution)/shard_map/ppermute | solution.py:24
  388.5 45.7 %collective-permute-start.24 = (bf16[512,1024]{1,0:T(8,128)(2,1)S(1)}, bf16[512,1024]{1,0:T(8,128)(2,1)S(1)}, u32[]{:S(2)}, u32[]{:S(2)}) collective-permute-start(bf16[512,1024]{1,0:T(8,128)(2,1)S(1)} %slice.522), channel_id=1, source_target_pairs={{0,2},{2,0},{4,6},{6,4},{8,10},{10,8},{12,14},{14,12},{16,18},{18,... | collective-permute-start | bytes 3145736 | tf_op jit(solution)/shard_map/ppermute | solution.py:12
  430.3 26.4 %collective-permute-start.26 = (bf16[4,128,1024]{2,1,0:T(8,128)(2,1)S(1)}, bf16[4,128,1024]{2,1,0:T(8,128)(2,1)S(1)}, u32[]{:S(2)}, u32[]{:S(2)}) collective-permute-start(bf16[4,128,1024]{2,1,0:T(8,128)(2,1)S(1)} %add_convert_fusion.2), channel_id=1, source_target_pairs={{0,4},{2,6},{4,0},{6,2},{8,12},{10,14},{12,8},{14,10},{16,20},{18,... | collective-permute-start | bytes 3145736 | tf_op jit(solution)/shard_map/ppermute | solution.py:12
  457.0 13.5 %collective-permute-start.27 = (bf16[2,128,1024]{2,1,0:T(8,128)(2,1)S(1)}, bf16[2,128,1024]{2,1,0:T(8,128)(2,1)S(1)}, u32[]{:S(2)}, u32[]{:S(2)}) collective-permute-start(bf16[2,128,1024]{2,1,0:T(8,128)(2,1)S(1)} %add_convert_fusion.9), channel_id=1, source_target_pairs={{0,8},{2,10},{4,12},{6,14},{8,0},{10,2},{12,4},{14,6},{16,24},{18,... | collective-permute-start | bytes 1572872 | tf_op jit(solution)/shard_map/ppermute | solution.py:12
  471.3 41.4 %collective-permute-start.28 = (bf16[1,128,1024]{2,1,0:T(8,128)(2,1)S(1)}, bf16[1,128,1024]{2,1,0:T(8,128)(2,1)S(1)}, u32[]{:S(2)}, u32[]{:S(2)}) collective-permute-start(bf16[1,128,1024]{2,1,0:T(8,128)(2,1)S(1)} %add_convert_fusion.13), channel_id=1, source_target_pairs={{0,16},{2,18},{4,20},{6,22},{8,24},{10,26},{12,28},{14,30},{16,0},... | collective-permute-start | bytes 786440 | tf_op jit(solution)/shard_map/ppermute | solution.py:12
  (65 other events, 660.7 us)
where the time goes:
time: 524 us; the launch traced here: 518 us
  waiting for transfers between devices  232 us (44%)
  matrix products  122 us (23%)
  other arithmetic  46 us (9%)
  blocking collectives  40.1 us (8%)
  local copies, waits for them, and re-layouts  38.7 us (7%)
  starting transfers between devices  36 us (7%)
    ppermute x34, waiting for transfers between devices, over_seq(): return lax.ppermute(block, 'seq', route)  144 us
    ppermute x8, waiting for transfers between devices, swap_pair(): return lax.ppermute(block, 'wshard', [(0, 1), (1, 0)])  88.6 us
    dot_general x9, matrix products, mm_nt(): lax.dot_general(left, right, (((1,), (1,)), ((), ())), preferred_element_...  50.2 us
    psum x1, blocking collectives, local(): lax.psum(jnp.concatenate([spread, grad_gain_mix[None], grad_gain_ffn[None...  40.1 us
    dot_general x9, matrix products, mm(): return jnp.dot(left, right, preferred_element_type=F32)  39.3 us
    dot_general x5, matrix products, mm_tn(): lax.dot_general(left, right, (((0,), (0,)), ((), ())), preferred_element_...  32.9 us
    ppermute x34, starting transfers between devices, over_seq(): return lax.ppermute(block, 'seq', route)  26.3 us
    unnamed x125, local copies, waits for them, and re-layouts  18.5 us
  transfers between devices with their start and end apart: 42, of which 15 were waited for; matrix products, arithmetic and copies ran while one was open for 33% of the time, Pallas kernels for 0%

commit v1 on v0

--- a/solution.py
+++ b/solution.py
@@ -6,6 +6,10 @@
 EPS = 1e-05
 LOW = jnp.bfloat16
 F32 = jnp.float32
+
+
+def derive_blocks_over_axis(v0):
+    return lax.all_gather(v0, ("seq", "wshard")).sum(axis=0)
 
 
 def over_seq(block, route):
@@ -344,9 +348,8 @@
     spread = lax.dynamic_update_slice_in_dim(
         spread, grad_taps[:, features:], (1 - pair) * half_width + core * features, 1
     )
-    sums = lax.psum(
-        jnp.concatenate([spread, grad_gain_mix[None], grad_gain_ffn[None]], axis=0),
-        ("seq", "wshard"),
+    sums = derive_blocks_over_axis(
+        jnp.concatenate([spread, grad_gain_mix[None], grad_gain_ffn[None]], axis=0)
     )
     sums = lax.dynamic_slice_in_dim(sums, pair * half_width, half_width, 1)
     return (

time: 524 us -> 555 us (1.059)
  blocking collectives: 40.1 us -> 72.7 us
    all_gather x0 -> x1, blocking collectives: none -> 72.7 us  [derive_blocks_over_axis(): return lax.all_gather(v0, ('seq', 'wshard')).sum(axis=0)]
    psum x1 -> x0, blocking collectives: 40.1 us -> none  [local(): lax.psum(jnp.concatenate([spread, grad_gain_mix[None], grad_gain_ffn[None...]
  transfers between devices with their start and end apart: 42 -> 42, of which waited for: 15 -> 15; matrix products, arithmetic and copies ran while one was open for 33% -> 34% of each run, Pallas kernels for 0% -> 0%
where the time goes in v1:
time: 555 us; the launch traced here: 548 us
  waiting for transfers between devices  230 us (41%)
  matrix products  122 us (22%)
  blocking collectives  72.7 us (13%)
  other arithmetic  46.1 us (8%)
  local copies, waits for them, and re-layouts  38.7 us (7%)
  starting transfers between devices  36.1 us (7%)
    ppermute x34, waiting for transfers between devices, over_seq(): return lax.ppermute(block, 'seq', route)  144 us
    ppermute x8, waiting for transfers between devices, swap_pair(): return lax.ppermute(block, 'wshard', [(0, 1), (1, 0)])  85.6 us
    all_gather x1, blocking collectives, derive_blocks_over_axis(): return lax.all_gather(v0, ('seq', 'wshard')).sum(axis=0)  72.7 us
    dot_general x9, matrix products, mm_nt(): lax.dot_general(left, right, (((1,), (1,)), ((), ())), preferred_element_...  50.2 us
    dot_general x9, matrix products, mm(): return jnp.dot(left, right, preferred_element_type=F32)  39.3 us
    dot_general x5, matrix products, mm_tn(): lax.dot_general(left, right, (((0,), (0,)), ((), ())), preferred_element_...  32.9 us
    ppermute x34, starting transfers between devices, over_seq(): return lax.ppermute(block, 'seq', route)  26.4 us
    unnamed x125, local copies, waits for them, and re-layouts  18.5 us
  transfers between devices with their start and end apart: 42, of which 15 were waited for; matrix products, arithmetic and copies ran while one was open for 34% of the time, Pallas kernels for 0%

profile of v1, /device:TPU:0, one launch (start us, length us, event | category | flops | bytes accessed | tf_op | source)
XLA Modules:
  0.0 548.3 jit_solution(3735923072541297260)
XLA Ops:
  12.7 4.7 collective-permute-start.7
  21.6 25.2 %collective-permute-done.1 = bf16[5,512]{1,0:T(8,128)(2,1)S(1)} collective-permute-done((bf16[5,512]{1,0:T(8,128)(2,1)S(1)}, bf16[5,512]{1,0:T(8,128)(2,1)S(1)}, u32[]{:S(2)}, u32[]{:S(2)}) %collective-permute-start.1) | collective-permute-done | bytes 5152 | tf_op jit(solution)/shard_map/ppermute | solution.py:28
  63.7 5.4 fusion.73
  73.1 4.2 convolution_convert_fusion.4
  79.7 23.4 %collective-permute-done.17 = bf16[512,1024]{1,0:T(8,128)(2,1)} collective-permute-done((bf16[512,1024]{1,0:T(8,128)(2,1)}, bf16[512,1024]{1,0:T(8,128)(2,1)}, u32[]{:S(2)}, u32[]{:S(2)}) %collective-permute-start.17) | collective-permute-done | bytes 1048608 | tf_op jit(solution)/shard_map/ppermute | solution.py:28
  113.5 4.5 fusion.61
  118.0 4.5 fusion.69
  122.6 9.7 %multiply_convert_fusion.2 = (bf16[1024,1152]{1,0:T(8,128)(2,1)S(1)}, bf16[1024,1152]{1,0:T(8,128)(2,1)}, bf16[1024,1152]{1,0:T(8,128)(2,1)}) fusion(f32[1024,1152]{1,0:T(8,128)} %fusion.69, f32[1024,1152]{1,0:T(8,128)} %fusion.61, bf16[2304,1024]{1,0:T(8,128)(2,1)S(1)} %bitcast.222, s32[]{:T(128)S(6)} %select_n.227, ...), kind=kOutput, calls=%fused_computation.14 | convolution fusion | flops 2437808128 | bytes 20971524 | tf_op jit(solution)/shard_map/dot_general | solution.py:44
  132.3 6.1 %fusion.65 = f32[1024,1024]{1,0:T(8,128)S(1)} fusion(bf16[1024,1152]{1,0:T(8,128)(2,1)} %get-tuple-element.24, bf16[1024,2304]{1,0:T(8,128)(2,1)} %param.16, s32[]{:T(128)S(6)} %select_n.227), kind=kOutput, calls=%fused_computation.113 | convolution fusion | flops 2415919104 | bytes 8912900 | tf_op jit(solution)/shard_map/dot_general | solution.py:44
  138.8 5.0 add_convert_fusion.1
  149.6 4.5 fusion.59
  154.1 4.5 fusion.67
  158.6 11.4 %multiply_convert_fusion = (bf16[1024,1152]{1,0:T(8,128)(2,1)S(1)}, bf16[1024,1152]{1,0:T(8,128)(2,1)}, bf16[1024,1152]{1,0:T(8,128)(2,1)}) fusion(f32[1024,1152]{1,0:T(8,128)} %fusion.67, f32[1024,1152]{1,0:T(8,128)} %fusion.59, bf16[2304,1024]{1,0:T(8,128)(2,1)} %param.18, s32[]{:T(128)S(6)} %select_n.227, bf16[512,1024]{1,0:T(8,128)(2,1)} %collective-permute-done.18, ...), kind=kOutput, calls=%fused_computation.12 | convolution fusion | flops 2437808128 | bytes 20971524 | tf_op jit(solution)/shard_map/dot_general | solution.py:44
  170.1 6.1 %convolution_convert_fusion.1 = bf16[1024,1024]{1,0:T(8,128)(2,1)S(1)} fusion(bf16[1024,1152]{1,0:T(8,128)(2,1)} %get-tuple-element.28, bf16[2304,1024]{1,0:T(8,128)(2,1)} %param.18, s32[]{:T(128)S(6)} %select_n.227), kind=kOutput, calls=%fused_computation.96 | convolution fusion | flops 2416967680 | bytes 6815748 | tf_op jit(solution)/shard_map/dot_general | solution.py:36
  177.6 4.6 fusion.63
  187.7 9.3 %fusion.21 = bf16[1024,1152]{1,0:T(8,128)(2,1)S(1)} fusion(bf16[1024,1152]{1,0:T(8,128)(2,1)} %get-tuple-element.28, bf16[1024,1152]{1,0:T(8,128)(2,1)} %get-tuple-element.25, bf16[512,1024]{1,0:T(8,128)(2,1)} %collective-permute-done.18, bf16[512,1024]{1,0:T(8,128)(2,1)} %collective-permute-done.17, bf16[512,1024]{1,0:T(8,128)(2,1)} %collective-permute-done.15, ...), kind=kOutput, calls=%fused_computation.37 | convolution fusion | flops 4859232256 | bytes 11272192 | tf_op jit(solution)/shard_map/dot_general | solution.py:40
  199.9 8.2 %fusion.26 = bf16[1024,1152]{1,0:T(8,128)(2,1)S(1)} fusion(bf16[1024,1152]{1,0:T(8,128)(2,1)} %copy-done.38, bf16[1024,1152]{1,0:T(8,128)(2,1)} %copy-done.37, bf16[512,1024]{1,0:T(8,128)(2,1)S(1)} %collective-permute-done.12, bf16[512,1024]{1,0:T(8,128)(2,1)S(1)} %collective-permute-done.11, bf16[1024,1024]{1,0:T(8,128)(2,1)S(1)} %multiply_convert_fusion.6), kind=kOutput, calls=%fused_computation.38 | convolution fusion | flops 4855037952 | bytes 11272192 | tf_op jit(solution)/shard_map/dot_general | solution.py:40
  210.2 8.8 %fusion.29 = bf16[1024,1152]{1,0:T(8,128)(2,1)S(1)} fusion(bf16[1024,1152]{1,0:T(8,128)(2,1)} %get-tuple-element.27, bf16[1024,1152]{1,0:T(8,128)(2,1)} %get-tuple-element.24, bf16[512,1024]{1,0:T(8,128)(2,1)} %copy-done.24, bf16[512,1024]{1,0:T(8,128)(2,1)} %copy-done.23, bf16[1024,1024]{1,0:T(8,128)(2,1)S(1)} %multiply_convert_fusion.6), kind=kOutput, calls=%fused_computation.39 | convolution fusion | flops 4855037952 | bytes 11272192 | tf_op jit(solution)/shard_map/dot_general | solution.py:40
  229.3 23.5 %collective-permute-done.34 = bf16[4,128,1152]{2,1,0:T(8,128)(2,1)} collective-permute-done((bf16[4,128,1152]{2,1,0:T(8,128)(2,1)}, bf16[4,128,1152]{2,1,0:T(8,128)(2,1)}, u32[]{:S(2)}, u32[]{:S(2)}) %collective-permute-start.34) | collective-permute-done | bytes 1179680 | tf_op jit(solution)/shard_map/ppermute | solution.py:16
  255.6 21.7 %collective-permute-done.30 = bf16[4,128,1152]{2,1,0:T(8,128)(2,1)S(1)} collective-permute-done((bf16[4,128,1152]{2,1,0:T(8,128)(2,1)S(1)}, bf16[4,128,1152]{2,1,0:T(8,128)(2,1)S(1)}, u32[]{:S(2)}, u32[]{:S(2)}) %collective-permute-start.30) | collective-permute-done | bytes 1179680 | tf_op jit(solution)/shard_map/ppermute | solution.py:16
  280.6 12.9 %collective-permute-done.35 = bf16[2,128,1152]{2,1,0:T(8,128)(2,1)S(1)} collective-permute-done((bf16[2,128,1152]{2,1,0:T(8,128)(2,1)S(1)}, bf16[2,128,1152]{2,1,0:T(8,128)(2,1)S(1)}, u32[]{:S(2)}, u32[]{:S(2)}) %collective-permute-start.35) | collective-permute-done | bytes 589856 | tf_op jit(solution)/shard_map/ppermute | solution.py:16
  295.3 9.3 %collective-permute-done.31 = bf16[2,128,1152]{2,1,0:T(8,128)(2,1)S(1)} collective-permute-done((bf16[2,128,1152]{2,1,0:T(8,128)(2,1)S(1)}, bf16[2,128,1152]{2,1,0:T(8,128)(2,1)S(1)}, u32[]{:S(2)}, u32[]{:S(2)}) %collective-permute-start.31) | collective-permute-done | bytes 589856 | tf_op jit(solution)/shard_map/ppermute | solution.py:16
  307.3 11.9 %collective-permute-done.40 = bf16[1,128,1152]{2,1,0:T(8,128)(2,1)S(1)} collective-permute-done((bf16[1,128,1152]{2,1,0:T(8,128)(2,1)S(1)}, bf16[1,128,1152]{2,1,0:T(8,128)(2,1)S(1)}, u32[]{:S(2)}, u32[]{:S(2)}) %collective-permute-start.40) | collective-permute-done | bytes 294944 | tf_op jit(solution)/shard_map/ppermute | solution.py:16
  320.3 14.0 %collective-permute-done.36 = bf16[1,128,1152]{2,1,0:T(8,128)(2,1)S(1)} collective-permute-done((bf16[1,128,1152]{2,1,0:T(8,128)(2,1)S(1)}, bf16[1,128,1152]{2,1,0:T(8,128)(2,1)S(1)}, u32[]{:S(2)}, u32[]{:S(2)}) %collective-permute-start.36) | collective-permute-done | bytes 294944 | tf_op jit(solution)/shard_map/ppermute | solution.py:16
  336.8 11.6 %collective-permute-done.32 = bf16[1,128,1152]{2,1,0:T(8,128)(2,1)S(1)} collective-permute-done((bf16[1,128,1152]{2,1,0:T(8,128)(2,1)S(1)}, bf16[1,128,1152]{2,1,0:T(8,128)(2,1)S(1)}, u32[]{:S(2)}, u32[]{:S(2)}) %collective-permute-start.32) | collective-permute-done | bytes 294944 | tf_op jit(solution)/shard_map/ppermute | solution.py:16
  349.6 4.0 fusion.122
  364.3 4.6 multiply_reduce_fusion.6
  375.1 3.7 convolution_convert_fusion
  391.0 37.0 %collective-permute-done.25 = bf16[8,128,1024]{2,1,0:T(8,128)(2,1)S(1)} collective-permute-done((bf16[8,128,1024]{2,1,0:T(8,128)(2,1)S(1)}, bf16[8,128,1024]{2,1,0:T(8,128)(2,1)S(1)}, u32[]{:S(2)}, u32[]{:S(2)}) %collective-permute-start.25) | collective-permute-done | bytes 2097184 | tf_op jit(solution)/shard_map/ppermute | solution.py:28
  432.3 22.5 %collective-permute-done.26 = bf16[4,128,1024]{2,1,0:T(8,128)(2,1)S(1)} collective-permute-done((bf16[4,128,1024]{2,1,0:T(8,128)(2,1)S(1)}, bf16[4,128,1024]{2,1,0:T(8,128)(2,1)S(1)}, u32[]{:S(2)}, u32[]{:S(2)}) %collective-permute-start.26) | collective-permute-done | bytes 1048608 | tf_op jit(solution)/shard_map/ppermute | solution.py:16
  457.3 11.3 %collective-permute-done.27 = bf16[2,128,1024]{2,1,0:T(8,128)(2,1)S(1)} collective-permute-done((bf16[2,128,1024]{2,1,0:T(8,128)(2,1)S(1)}, bf16[2,128,1024]{2,1,0:T(8,128)(2,1)S(1)}, u32[]{:S(2)}, u32[]{:S(2)}) %collective-permute-start.27) | collective-permute-done | bytes 524320 | tf_op jit(solution)/shard_map/ppermute | solution.py:16
  469.4 72.7 %all-gather.1 = f32[32,5,1024]{2,1,0:T(8,128)S(1)} all-gather(f32[1,5,1024]{2,1,0:T(8,128)S(1)} %maximum_bitcast_fusion), channel_id=2, replica_groups=mesh['seq'=16,'wshard'=2] {'seq','wshard'}, dimensions={0}, use_global_device_ids=true | all-gather | bytes 675840 | tf_op jit(solution)/shard_map/all_gather | solution.py:12
  (343 shorter events, 135.3 us)
Async XLA Ops:
  5.7 41.8 %collective-permute-start.5 = (bf16[4,2,1152]{2,0,1:T(4,128)(2,1)S(1)}, bf16[4,2,1152]{2,0,1:T(4,128)(2,1)S(1)}, u32[]{:S(2)}, u32[]{:S(2)}) collective-permute-start(bf16[4,2,1152]{2,0,1:T(4,128)(2,1)S(1)} %get-tuple-element.69), channel_id=1, source_target_pairs={{4,0},{8,4},{12,8},{16,12},{20,16},{24,20},{28,24},{5,1},{9,5},{13... | collective-permute-start | bytes 55304 | tf_op jit(solution)/shard_map/ppermute | solution.py:16
  7.0 41.0 %collective-permute-start.6 = (bf16[4,2,1152]{2,0,1:T(4,128)(2,1)S(1)}, bf16[4,2,1152]{2,0,1:T(4,128)(2,1)S(1)}, u32[]{:S(2)}, u32[]{:S(2)}) collective-permute-start(bf16[4,2,1152]{2,0,1:T(4,128)(2,1)S(1)} %get-tuple-element.69), channel_id=1, source_target_pairs={{4,2},{8,6},{12,10},{16,14},{20,18},{24,22},{28,26},{5,3},{9,7},{1... | collective-permute-start | bytes 55304 | tf_op jit(solution)/shard_map/ppermute | solution.py:16
  9.0 42.0 %collective-permute-start.2 = (bf16[3,1024,256]{2,1,0:T(8,128)(2,1)}, bf16[3,1024,256]{2,1,0:T(8,128)(2,1)}, u32[]{:S(2)}, u32[]{:S(2)}) collective-permute-start(bf16[3,1024,256]{2,1,0:T(8,128)(2,1)} %dynamic-slice_bitcast_fusion), channel_id=1, source_target_pairs={{0,1},{1,0},{2,3},{3,2},{4,5},{5,4},{6,7},{7,6},{8,9},{9,8},{10,11... | collective-permute-start | bytes 4718600 | tf_op jit(solution)/shard_map/ppermute | solution.py:28
  11.9 37.5 %collective-permute-start.3 = (bf16[4,2,1152]{2,0,1:T(4,128)(2,1)S(1)}, bf16[4,2,1152]{2,0,1:T(4,128)(2,1)S(1)}, u32[]{:S(2)}, u32[]{:S(2)}) collective-permute-start(bf16[4,2,1152]{2,0,1:T(4,128)(2,1)S(1)} %get-tuple-element.68), channel_id=1, source_target_pairs={{2,4},{6,8},{10,12},{14,16},{18,20},{22,24},{26,28},{3,5},{7,9},{1... | collective-permute-start | bytes 55304 | tf_op jit(solution)/shard_map/ppermute | solution.py:16
  21.3 25.4 %collective-permute-start.1 = (bf16[5,512]{1,0:T(8,128)(2,1)S(1)}, bf16[5,512]{1,0:T(8,128)(2,1)S(1)}, u32[]{:S(2)}, u32[]{:S(2)}) collective-permute-start(bf16[5,512]{1,0:T(8,128)(2,1)S(1)} %pad_maximum_fusion.25), channel_id=1, source_target_pairs={{0,1},{1,0},{2,3},{3,2},{4,5},{5,4},{6,7},{7,6},{8,9},{9,8},{10,11... | collective-permute-start | bytes 15368 | tf_op jit(solution)/shard_map/ppermute | solution.py:28
  48.0 25.1 %collective-permute-start.8 = (bf16[256,1024]{1,0:T(8,128)(2,1)}, bf16[256,1024]{1,0:T(8,128)(2,1)}, u32[]{:S(2)}, u32[]{:S(2)}) collective-permute-start(bf16[256,1024]{1,0:T(8,128)(2,1)} %constant_dynamic-slice_fusion.25), channel_id=1, source_target_pairs={{0,1},{1,0},{2,3},{3,2},{4,5},{5,4},{6,7},{7,6},{8,9},{9,8},{10,11... | collective-permute-start | bytes 1572872 | tf_op jit(solution)/shard_map/ppermute | solution.py:28
  77.2 29.5 %collective-permute-start.9 = (bf16[1024,1024]{1,0:T(8,128)(2,1)}, bf16[1024,1024]{1,0:T(8,128)(2,1)}, u32[]{:S(2)}, u32[]{:S(2)}) collective-permute-start(bf16[1024,1024]{1,0:T(8,128)(2,1)} %convolution_convert_fusion.4), channel_id=1, source_target_pairs={{0,2},{2,0},{4,6},{6,4},{8,10},{10,8},{12,14},{14,12},{16,18},{18,... | collective-permute-start | bytes 6291464 | tf_op jit(solution)/shard_map/ppermute | solution.py:16
  77.5 25.7 %collective-permute-start.17 = (bf16[512,1024]{1,0:T(8,128)(2,1)}, bf16[512,1024]{1,0:T(8,128)(2,1)}, u32[]{:S(2)}, u32[]{:S(2)}) collective-permute-start(bf16[512,1024]{1,0:T(8,128)(2,1)} %bitcast.18), channel_id=1, source_target_pairs={{0,1},{1,0},{2,3},{3,2},{4,5},{5,4},{6,7},{7,6},{8,9},{9,8},{10,11... | collective-permute-start | bytes 3145736 | tf_op jit(solution)/shard_map/ppermute | solution.py:28
  78.9 43.6 %collective-permute-start.15 = (bf16[512,1024]{1,0:T(8,128)(2,1)}, bf16[512,1024]{1,0:T(8,128)(2,1)}, u32[]{:S(2)}, u32[]{:S(2)}) collective-permute-start(bf16[512,1024]{1,0:T(8,128)(2,1)} %bitcast.18), channel_id=1, source_target_pairs={{0,2},{2,0},{4,6},{6,4},{8,10},{10,8},{12,14},{14,12},{16,18},{18,... | collective-permute-start | bytes 3145736 | tf_op jit(solution)/shard_map/ppermute | solution.py:16
  103.1 55.5 %collective-permute-start.18 = (bf16[512,1024]{1,0:T(8,128)(2,1)}, bf16[512,1024]{1,0:T(8,128)(2,1)}, u32[]{:S(2)}, u32[]{:S(2)}) collective-permute-start(bf16[512,1024]{1,0:T(8,128)(2,1)} %collective-permute-done.17), channel_id=1, source_target_pairs={{0,2},{2,0},{4,6},{6,4},{8,10},{10,8},{12,14},{14,12},{16,18},{18,... | collective-permute-start | bytes 3145736 | tf_op jit(solution)/shard_map/ppermute | solution.py:16
  111.9 26.5 %collective-permute-start.11 = (bf16[512,1024]{1,0:T(8,128)(2,1)S(1)}, bf16[512,1024]{1,0:T(8,128)(2,1)S(1)}, u32[]{:S(2)}, u32[]{:S(2)}) collective-permute-start(bf16[512,1024]{1,0:T(8,128)(2,1)S(1)} %slice.503), channel_id=1, source_target_pairs={{0,1},{1,0},{2,3},{3,2},{4,5},{5,4},{6,7},{7,6},{8,9},{9,8},{10,11... | collective-permute-start | bytes 3145736 | tf_op jit(solution)/shard_map/ppermute | solution.py:28
  144.8 203.8 %collective-permute-start.16 = (bf16[512,1024]{1,0:T(8,128)(2,1)}, bf16[512,1024]{1,0:T(8,128)(2,1)S(1)}, u32[]{:S(2)}, u32[]{:S(2)}) collective-permute-start(bf16[512,1024]{1,0:T(8,128)(2,1)} %slice.507), channel_id=1, source_target_pairs={{0,2},{2,0},{4,6},{6,4},{8,10},{10,8},{12,14},{14,12},{16,18},{18,... | collective-permute-start | bytes 3145736 | tf_op jit(solution)/shard_map/ppermute | solution.py:16
  177.3 42.1 %collective-permute-start.13 = (bf16[512,1024]{1,0:T(8,128)(2,1)}, bf16[512,1024]{1,0:T(8,128)(2,1)}, u32[]{:S(2)}, u32[]{:S(2)}) collective-permute-start(bf16[512,1024]{1,0:T(8,128)(2,1)} %slice.505), channel_id=1, source_target_pairs={{0,2},{2,0},{4,6},{6,4},{8,10},{10,8},{12,14},{14,12},{16,18},{18,... | collective-permute-start | bytes 3145736 | tf_op jit(solution)/shard_map/ppermute | solution.py:16
  187.4 35.1 %collective-permute-start.19 = (bf16[512,1024]{1,0:T(8,128)(2,1)}, bf16[512,1024]{1,0:T(8,128)(2,1)}, u32[]{:S(2)}, u32[]{:S(2)}) collective-permute-start(bf16[512,1024]{1,0:T(8,128)(2,1)} %slice.509), channel_id=1, source_target_pairs={{0,2},{2,0},{4,6},{6,4},{8,10},{10,8},{12,14},{14,12},{16,18},{18,... | collective-permute-start | bytes 3145736 | tf_op jit(solution)/shard_map/ppermute | solution.py:16
  198.4 29.1 %collective-permute-start.38 = (bf16[4,128,1152]{2,1,0:T(8,128)(2,1)}, bf16[4,128,1152]{2,1,0:T(8,128)(2,1)}, u32[]{:S(2)}, u32[]{:S(2)}) collective-permute-start(bf16[4,128,1152]{2,1,0:T(8,128)(2,1)} %pad_maximum_fusion.16), channel_id=1, source_target_pairs={{0,4},{2,6},{4,0},{6,2},{8,12},{10,14},{12,8},{14,10},{16,20},{18,... | collective-permute-start | bytes 3538952 | tf_op jit(solution)/shard_map/ppermute | solution.py:16
  209.7 43.1 %collective-permute-start.34 = (bf16[4,128,1152]{2,1,0:T(8,128)(2,1)}, bf16[4,128,1152]{2,1,0:T(8,128)(2,1)}, u32[]{:S(2)}, u32[]{:S(2)}) collective-permute-start(bf16[4,128,1152]{2,1,0:T(8,128)(2,1)} %pad_maximum_fusion.15), channel_id=1, source_target_pairs={{0,4},{2,6},{4,0},{6,2},{8,12},{10,14},{12,8},{14,10},{16,20},{18,... | collective-permute-start | bytes 3538952 | tf_op jit(solution)/shard_map/ppermute | solution.py:16
  220.2 129.4 %collective-permute-start.10 = (bf16[512,1024]{1,0:T(8,128)(2,1)S(1)}, bf16[512,1024]{1,0:T(8,128)(2,1)S(1)}, u32[]{:S(2)}, u32[]{:S(2)}) collective-permute-start(bf16[512,1024]{1,0:T(8,128)(2,1)S(1)} %copy-done.22), channel_id=1, source_target_pairs={{0,2},{2,0},{4,6},{6,4},{8,10},{10,8},{12,14},{14,12},{16,18},{18,... | collective-permute-start | bytes 3145736 | tf_op jit(solution)/shard_map/ppermute | solution.py:16
  222.5 54.8 %collective-permute-start.30 = (bf16[4,128,1152]{2,1,0:T(8,128)(2,1)S(1)}, bf16[4,128,1152]{2,1,0:T(8,128)(2,1)S(1)}, u32[]{:S(2)}, u32[]{:S(2)}) collective-permute-start(bf16[4,128,1152]{2,1,0:T(8,128)(2,1)S(1)} %pad_maximum_fusion.14), channel_id=1, source_target_pairs={{0,4},{2,6},{4,0},{6,2},{8,12},{10,14},{12,8},{14,10},{16,20},{18,... | collective-permute-start | bytes 3538952 | tf_op jit(solution)/shard_map/ppermute | solution.py:16
  227.5 122.1 %collective-permute-start.14 = (bf16[512,1024]{1,0:T(8,128)(2,1)S(1)}, bf16[512,1024]{1,0:T(8,128)(2,1)S(1)}, u32[]{:S(2)}, u32[]{:S(2)}) collective-permute-start(bf16[512,1024]{1,0:T(8,128)(2,1)S(1)} %add_convert_fusion.5), channel_id=1, source_target_pairs={{0,1},{1,0},{2,3},{3,2},{4,5},{5,4},{6,7},{7,6},{8,9},{9,8},{10,11... | collective-permute-start | bytes 3145736 | tf_op jit(solution)/shard_map/ppermute | solution.py:28
  252.8 26.2 %collective-permute-start.39 = (bf16[2,128,1152]{2,1,0:T(8,128)(2,1)S(1)}, bf16[2,128,1152]{2,1,0:T(8,128)(2,1)S(1)}, u32[]{:S(2)}, u32[]{:S(2)}) collective-permute-start(bf16[2,128,1152]{2,1,0:T(8,128)(2,1)S(1)} %add_convert_fusion.6), channel_id=1, source_target_pairs={{0,8},{2,10},{4,12},{6,14},{8,0},{10,2},{12,4},{14,6},{16,24},{18,... | collective-permute-start | bytes 1769480 | tf_op jit(solution)/shard_map/ppermute | solution.py:16
  277.3 16.3 %collective-permute-start.35 = (bf16[2,128,1152]{2,1,0:T(8,128)(2,1)S(1)}, bf16[2,128,1152]{2,1,0:T(8,128)(2,1)S(1)}, u32[]{:S(2)}, u32[]{:S(2)}) collective-permute-start(bf16[2,128,1152]{2,1,0:T(8,128)(2,1)S(1)} %add_convert_fusion.7), channel_id=1, source_target_pairs={{0,8},{2,10},{4,12},{6,14},{8,0},{10,2},{12,4},{14,6},{16,24},{18,... | collective-permute-start | bytes 1769480 | tf_op jit(solution)/shard_map/ppermute | solution.py:16
  279.0 25.6 %collective-permute-start.31 = (bf16[2,128,1152]{2,1,0:T(8,128)(2,1)S(1)}, bf16[2,128,1152]{2,1,0:T(8,128)(2,1)S(1)}, u32[]{:S(2)}, u32[]{:S(2)}) collective-permute-start(bf16[2,128,1152]{2,1,0:T(8,128)(2,1)S(1)} %add_convert_fusion.8), channel_id=1, source_target_pairs={{0,8},{2,10},{4,12},{6,14},{8,0},{10,2},{12,4},{14,6},{16,24},{18,... | collective-permute-start | bytes 1769480 | tf_op jit(solution)/shard_map/ppermute | solution.py:16
  293.6 55.1 %collective-permute-start.20 = (bf16[512,1024]{1,0:T(8,128)(2,1)S(1)}, bf16[512,1024]{1,0:T(8,128)(2,1)S(1)}, u32[]{:S(2)}, u32[]{:S(2)}) collective-permute-start(bf16[512,1024]{1,0:T(8,128)(2,1)S(1)} %add_convert_fusion.3), channel_id=1, source_target_pairs={{0,1},{1,0},{2,3},{3,2},{4,5},{5,4},{6,7},{7,6},{8,9},{9,8},{10,11... | collective-permute-start | bytes 3145736 | tf_op jit(solution)/shard_map/ppermute | solution.py:28
  304.6 14.6 %collective-permute-start.40 = (bf16[1,128,1152]{2,1,0:T(8,128)(2,1)S(1)}, bf16[1,128,1152]{2,1,0:T(8,128)(2,1)S(1)}, u32[]{:S(2)}, u32[]{:S(2)}) collective-permute-start(bf16[1,128,1152]{2,1,0:T(8,128)(2,1)S(1)} %add_convert_fusion.10), channel_id=1, source_target_pairs={{0,16},{2,18},{4,20},{6,22},{8,24},{10,26},{12,28},{14,30},{16,0},... | collective-permute-start | bytes 884744 | tf_op jit(solution)/shard_map/ppermute | solution.py:16
  319.2 15.1 %collective-permute-start.36 = (bf16[1,128,1152]{2,1,0:T(8,128)(2,1)S(1)}, bf16[1,128,1152]{2,1,0:T(8,128)(2,1)S(1)}, u32[]{:S(2)}, u32[]{:S(2)}) collective-permute-start(bf16[1,128,1152]{2,1,0:T(8,128)(2,1)S(1)} %add_convert_fusion.11), channel_id=1, source_target_pairs={{0,16},{2,18},{4,20},{6,22},{8,24},{10,26},{12,28},{14,30},{16,0},... | collective-permute-start | bytes 884744 | tf_op jit(solution)/shard_map/ppermute | solution.py:16
  334.3 14.2 %collective-permute-start.32 = (bf16[1,128,1152]{2,1,0:T(8,128)(2,1)S(1)}, bf16[1,128,1152]{2,1,0:T(8,128)(2,1)S(1)}, u32[]{:S(2)}, u32[]{:S(2)}) collective-permute-start(bf16[1,128,1152]{2,1,0:T(8,128)(2,1)S(1)} %add_convert_fusion.12), channel_id=1, source_target_pairs={{0,16},{2,18},{4,20},{6,22},{8,24},{10,26},{12,28},{14,30},{16,0},... | collective-permute-start | bytes 884744 | tf_op jit(solution)/shard_map/ppermute | solution.py:16
  359.0 22.1 %collective-permute-start.37 = (bf16[64,1152]{1,0:T(8,128)(2,1)}, bf16[64,1152]{1,0:T(8,128)(2,1)}, u32[]{:S(2)}, u32[]{:S(2)}) collective-permute-start(bf16[64,1152]{1,0:T(8,128)(2,1)} %fusion.82), channel_id=1, source_target_pairs={{0,2},{2,0},{4,6},{6,4},{8,10},{10,8},{12,14},{14,12},{16,18},{18,... | collective-permute-start | bytes 442376 | tf_op jit(solution)/shard_map/ppermute | solution.py:16
  361.6 20.6 %collective-permute-start.33 = (bf16[64,1152]{1,0:T(8,128)(2,1)}, bf16[64,1152]{1,0:T(8,128)(2,1)}, u32[]{:S(2)}, u32[]{:S(2)}) collective-permute-start(bf16[64,1152]{1,0:T(8,128)(2,1)} %fusion.81), channel_id=1, source_target_pairs={{0,2},{2,0},{4,6},{6,4},{8,10},{10,8},{12,14},{14,12},{16,18},{18,... | collective-permute-start | bytes 442376 | tf_op jit(solution)/shard_map/ppermute | solution.py:16
  379.6 48.4 %collective-permute-start.25 = (bf16[8,128,1024]{2,1,0:T(8,128)(2,1)S(1)}, bf16[8,128,1024]{2,1,0:T(8,128)(2,1)S(1)}, u32[]{:S(2)}, u32[]{:S(2)}) collective-permute-start(bf16[8,128,1024]{2,1,0:T(8,128)(2,1)S(1)} %dynamic-slice_dynamic-update-slice_fusion), channel_id=1, source_target_pairs={{0,1},{1,0},{2,3},{3,2},{4,5},{5,4},{6,7},{7,6},{8,9},{9,8},{10,11... | collective-permute-start | bytes 6291464 | tf_op jit(solution)/shard_map/ppermute | solution.py:28
  388.5 42.9 %collective-permute-start.24 = (bf16[512,1024]{1,0:T(8,128)(2,1)S(1)}, bf16[512,1024]{1,0:T(8,128)(2,1)S(1)}, u32[]{:S(2)}, u32[]{:S(2)}) collective-permute-start(bf16[512,1024]{1,0:T(8,128)(2,1)S(1)} %slice.522), channel_id=1, source_target_pairs={{0,2},{2,0},{4,6},{6,4},{8,10},{10,8},{12,14},{14,12},{16,18},{18,... | collective-permute-start | bytes 3145736 | tf_op jit(solution)/shard_map/ppermute | solution.py:16
  428.4 26.4 %collective-permute-start.26 = (bf16[4,128,1024]{2,1,0:T(8,128)(2,1)S(1)}, bf16[4,128,1024]{2,1,0:T(8,128)(2,1)S(1)}, u32[]{:S(2)}, u32[]{:S(2)}) collective-permute-start(bf16[4,128,1024]{2,1,0:T(8,128)(2,1)S(1)} %add_convert_fusion.2), channel_id=1, source_target_pairs={{0,4},{2,6},{4,0},{6,2},{8,12},{10,14},{12,8},{14,10},{16,20},{18,... | collective-permute-start | bytes 3145736 | tf_op jit(solution)/shard_map/ppermute | solution.py:16
  469.4 74.1 %collective-permute-start.28 = (bf16[1,128,1024]{2,1,0:T(8,128)(2,1)S(1)}, bf16[1,128,1024]{2,1,0:T(8,128)(2,1)S(1)}, u32[]{:S(2)}, u32[]{:S(2)}) collective-permute-start(bf16[1,128,1024]{2,1,0:T(8,128)(2,1)S(1)} %add_convert_fusion.13), channel_id=1, source_target_pairs={{0,16},{2,18},{4,20},{6,22},{8,24},{10,26},{12,28},{14,30},{16,0},... | collective-permute-start | bytes 786440 | tf_op jit(solution)/shard_map/ppermute | solution.py:16
  (65 other events, 750.2 us)
